TPU v7x, 128 devices: a whole 4x4x4 slice. The times are simulated.
128 devices in a mesh: blk: 32 (over x, y, core), wid: 4 (over z).
Axes of the slice: x: 4, y: 4, z: 4, core: 2. Of those that a mesh axis runs over, the one named last changes fastest.
Arguments:
- queries: bfloat16 [7168, 4096], P('blk', 'wid'), may hold values from -30 to 30
- passages: bfloat16 [7168, 4096], P('blk', 'wid'), may hold values from -7 to 7
- pairs: int32 [32, 32], replicated, may hold values from 0 to 1, as said below
Outputs:
- loss: float32 [], replicated
- grad_queries: bfloat16 [7168, 4096], P('blk', 'wid')
- grad_passages: bfloat16 [7168, 4096], P('blk', 'wid')
Inputs may be any that keep to these rules, and one draw needn't show every extreme that they name: pairs is 0 on its diagonal; each query block lists its own number of hard-negative blocks, each at most once.
All inputs are finite; a program needn't handle non-finite values.
Results may differ from a plain program's by a relative error of at most 0.017.
Values may be sent and summed in bfloat16 or wider, within the bound.
A program may use at most 128 MiB of HBM per device.

v0:
```python
import jax
import jax.numpy as jnp
from jax import lax
from jax.sharding import PartitionSpec as P


def softmax_weights(scores, colmask, pos_cols):
    masked = jnp.where(colmask[None, :], scores, -jnp.inf)
    highest = jnp.max(masked, axis=1, keepdims=True)
    expon = jnp.exp(masked - highest)
    totals = jnp.sum(expon, axis=1, keepdims=True)
    log_total = highest[:, 0] + jnp.log(totals[:, 0])
    onehot = jnp.arange(scores.shape[1], dtype=jnp.int32)[None, :] == pos_cols[:, None]
    positive = jnp.sum(jnp.where(onehot, scores, 0.0), axis=1)
    prob = expon / totals
    weights = (prob - onehot.astype(jnp.float32)).astype(jnp.bfloat16)
    return (weights, jnp.sum(log_total - positive))


def body(queries, passages, pairs):
    block_rows = queries.shape[0]
    width_cols = queries.shape[1]
    blocks = lax.axis_size("blk")
    width_parts = lax.axis_size("wid")
    my_block = lax.axis_index("blk")
    score_scale = (width_cols * width_parts) ** (-0.5)
    pair_row = lax.dynamic_slice_in_dim(pairs, my_block, 1, 0)[0]
    allowed = (pair_row == 1) | (jnp.arange(blocks, dtype=jnp.int32) == my_block)
    colmask = jnp.repeat(allowed, block_rows)
    gathered = lax.all_gather(passages, "blk", axis=0, tiled=True)
    partial_value = lax.dot_general(
        queries, gathered, (((1,), (1,)), ((), ())), preferred_element_type=jnp.float32
    )
    scores = lax.psum(partial_value, "wid") * score_scale
    pos_cols = my_block * block_rows + jnp.arange(block_rows, dtype=jnp.int32)
    weights, loss_part = softmax_weights(scores, colmask, pos_cols)
    loss = lax.psum(loss_part, "blk") / (blocks * block_rows)
    grad_rows = jnp.dot(weights, gathered, preferred_element_type=jnp.float32)
    grad_pass = lax.psum_scatter(
        lax.dot_general(
            weights, queries, (((0,), (0,)), ((), ())), preferred_element_type=jnp.float32
        ).astype(jnp.bfloat16),
        "blk",
        scatter_dimension=0,
        tiled=True,
    )
    return (loss, grad_rows.astype(jnp.bfloat16), grad_pass)


def solution(mesh):
    return jax.shard_map(
        body,
        mesh=mesh,
        in_specs=(P("blk", "wid"), P("blk", "wid"), P()),
        out_specs=(P(), P("blk", "wid"), P("blk", "wid")),
        check_vma=False,
    )
```

profile of v0, /device:TPU:1, one launch (start us, length us, event | category | flops | bytes accessed | tf_op | source)
XLA Modules:
  0.0 359.5 jit_solution(15625718289489157599)
XLA Ops:
  7.2 0.0 copy-start
  7.2 0.0 all-gather.2.cloned.1.call-start
  7.2 0.7 all-gather.2.cloned.1.call-update
  7.9 0.0 all-reduce.2.cloned.1.call-start
  8.0 73.6 %all-gather.2.cloned.1.call-done = bf16[7168,1024]{1,0:T(8,128)(2,1)} async-done(((bf16[224,1024]{1,0:T(8,128)(2,1)}), bf16[7168,1024]{1,0:T(8,128)(2,1)}) %all-gather.2.cloned.1.call-update) | async-done | bytes 14680080 | tf_op jit(solution)/shard_map/all_gather | solution.py:30
  81.6 0.0 copy-done
  81.6 12.3 %fusion.1 = f32[224,7168]{1,0:T(8,128)} fusion(bf16[224,1024]{1,0:T(8,128)(2,1)S(1)} %copy-done, bf16[7168,1024]{1,0:T(8,128)(2,1)} %all-gather.2.cloned.1.call-done), kind=kOutput, calls=%fused_computation.11 | convolution fusion | flops 3288334336 | bytes 21561344 | tf_op jit(solution)/shard_map/dot_general | solution.py:31
  93.9 0.0 all-reduce.2.cloned.1.call-update
  93.9 0.2 reduce-scatter.2.cloned.1.call-start
  94.1 0.7 bitcast_or_fusion
  94.8 0.1 broadcast_in_dim.25
  94.9 0.1 broadcast_in_dim.26
  95.0 127.4 %all-reduce.2.cloned.1.call-done = f32[224,7168]{1,0:T(8,128)} async-done(((f32[224,7168]{1,0:T(8,128)}), f32[224,7168]{1,0:T(8,128)}) %all-reduce.2.cloned.1.call-update) | async-done | bytes 6422544 | tf_op jit(solution)/shard_map/psum | solution.py:34
  222.4 0.0 copy-start.1
  222.4 3.9 %select_reduce_fusion.1 = f32[224]{0:T(256)S(1)} fusion(f32[224,7168]{1,0:T(8,128)} %all-reduce.2.cloned.1.call-done, pred[7168]{0:T(1024)(128)(4,1)S(1)} %broadcast_in_dim.26), kind=kLoop, calls=%fused_computation.5 | loop fusion | flops 4816672 | bytes 6430592 | tf_op jit(solution)/shard_map/reduce_max | solution.py:9
  226.3 0.8 copy-done.1
  227.1 3.0 fusion
  230.1 13.4 %convolution_convert_fusion = bf16[7168,1024]{1,0:T(8,128)(2,1)} fusion(bf16[224,1024]{1,0:T(8,128)(2,1)S(1)} %copy-done, f32[224,7168]{1,0:T(8,128)} %all-reduce.2.cloned.1.call-done, f32[224]{0:T(256)S(1)} %get-tuple-element.3, s32[224]{0:T(256)S(1)} %iota_add_fusion, f32[224]{0:T(256)S(1)} %select_reduce_fusion.1, pred[7168]{0:T(1024)(128)(4,1)S(1)} %broadcast_in_dim.26), kind=kOutput, calls=%fused_computation | convolution fusion | flops 3308519424 | bytes 21571200 | tf_op jit(solution)/shard_map/dot_general | solution.py:40
  243.5 0.0 reduce-scatter.2.cloned.1.call-update
  243.5 0.6 subtract_reduce_fusion
  244.1 63.8 %psum.15 = f32[]{:T(128)} all-reduce(f32[]{:T(128)} %subtract_reduce_fusion), channel_id=1, replica_groups=mesh['blk'=32,'wid'=4] {'blk'}, use_global_device_ids=true, to_apply=%region_5.6 | all-reduce | flops 1 | bytes 8 | tf_op jit(solution)/shard_map/psum | solution.py:37
  308.5 12.4 %convolution_convert_fusion.1 = bf16[224,1024]{1,0:T(8,128)(2,1)} fusion(bf16[7168,1024]{1,0:T(8,128)(2,1)} %all-gather.2.cloned.1.call-done, f32[224,7168]{1,0:T(8,128)} %all-reduce.2.cloned.1.call-done, f32[224]{0:T(256)S(1)} %get-tuple-element.3, s32[224]{0:T(256)S(1)} %iota_add_fusion, f32[224]{0:T(256)S(1)} %select_reduce_fusion.1, ...), kind=kOutput, calls=%fused_computation.7 | convolution fusion | flops 3301408768 | bytes 21571200 | tf_op jit(solution)/shard_map/dot_general | solution.py:38
  321.0 30.9 %reduce-scatter.2.cloned.1.call-done = bf16[224,1024]{1,0:T(8,128)(2,1)} async-done(((bf16[7168,1024]{1,0:T(8,128)(2,1)}), bf16[224,1024]{1,0:T(8,128)(2,1)}) %reduce-scatter.2.cloned.1.call-update) | async-done | bytes 458768 | tf_op jit(solution)/shard_map/reduce_scatter | solution.py:39
  (1 shorter events, 0.0 us)
Async XLA Ops:
  7.2 74.4 %copy-start = (bf16[224,1024]{1,0:T(8,128)(2,1)S(1)}, bf16[224,1024]{1,0:T(8,128)(2,1)}, u32[]{:S(2)}) copy-start(bf16[224,1024]{1,0:T(8,128)(2,1)} %param.3) | copy-start | bytes 1376260
  7.2 74.4 %all-gather.2.cloned.1.call-start = ((), (), s32[]{:S(2)}) async-start(), calls=%async_computation.1 | async-start | bytes 15138816 | tf_op jit(solution)/shard_map/all_gather | solution.py:30
  7.9 214.5 %all-reduce.2.cloned.1.call-start = ((), (), s32[]{:S(2)}) async-start(), calls=%async_computation.2 | async-start | bytes 12845056 | tf_op jit(solution)/shard_map/psum | solution.py:34
  93.9 258.0 %reduce-scatter.2.cloned.1.call-start = ((), (), s32[]{:S(2)}) async-start(), calls=%async_computation.3 | async-start | bytes 15138816 | tf_op jit(solution)/shard_map/reduce_scatter | solution.py:39
  222.4 4.7 %copy-start.1 = (f32[224,7168]{1,0:T(8,128)S(1)}, f32[224,7168]{1,0:T(8,128)}, u32[]{:S(2)}) copy-start(f32[224,7168]{1,0:T(8,128)} %all-reduce.2.cloned.1.call-done) | copy-start | bytes 19267588
Sparse Core Ops, SparseCore 0:
  10.3 71.2 all-gather.1
  94.0 128.3 all-reduce.1
  243.6 108.2 reduce-scatter.1
where the time goes:
time: 360 us
  waiting for transfers between devices  233 us (65%)
  blocking collectives  63.8 us (18%)
  matrix products  38.1 us (11%)
  between operations  15.6 us (4%)
  other arithmetic  8.15 us (2%)
    psum x1, waiting for transfers between devices, body(): scores = lax.psum(partial_value, 'wid') * score_scale  127 us
    all_gather x1, waiting for transfers between devices, body(): gathered = lax.all_gather(passages, 'blk', axis=0, tiled=True)  73.6 us
    psum x1, blocking collectives, body(): loss = lax.psum(loss_part, 'blk') / (blocks * block_rows)  63.8 us
    reduce_scatter x1, waiting for transfers between devices, body(): lax.psum_scatter(lax.dot_general(weights, queries, (((0,), (0,)), ((), ()...  30.9 us
    dot_general x1, matrix products, body(): lax.dot_general(weights, queries, (((0,), (0,)), ((), ())), preferred_ele...  13.4 us
    dot_general x1, matrix products, body(): grad_rows = jnp.dot(weights, gathered, preferred_element_type=jnp.float32)  12.4 us
    dot_general x1, matrix products, body(): lax.dot_general(queries, gathered, (((1,), (1,)), ((), ())), preferred_el...  12.3 us
  transfers between devices with their start and end apart: 3, of which 3 were waited for; matrix products, arithmetic and copies ran while one was open for 4% of the time, Pallas kernels for 0%

commit v1 on v0

v1 whole, which is shorter than its diff:
```python
import jax
import jax.numpy as jnp
from jax import lax
from jax.experimental import pallas as pl
from jax.experimental.pallas import tpu as pltpu
from jax.sharding import PartitionSpec as P

MESH = pl.DeviceIdType.MESH
BR = 224
HALF = BR // 2
WC = 512
TILE = 4 * BR
CORE = 2 * BR
SUB = 32
NEG = -1e30
SCALE = 4096 ** -0.5
ORDER_IN = ((0, 1, 3, 2), (0, 3, 1, 2))
ORDER_OUT = ((2, 1, 3, 0), (2, 3, 1, 0))
F32 = jnp.float32
BF16 = jnp.bfloat16


def rows(slot, n=BR, off=0):
    return pl.ds(pl.multiple_of(slot * BR + off, 16), n)


def kernel(
    q_hbm, p_hbm, pairs_ref, loss_ref, gq_ref, gp_ref,
    qg, pg, tile, tile_in, wp, wq, st_f, in_f, st_n, in_n, st_z, in_z, stat, stats, lossv, losses,
    r1, s1, rn, sn, rf, sf, rt, sst, rst, sstat, rw, sw, rf5, sf5, rn5, sn5, rz, sz, rl, sl,
):
    blk = lax.axis_index("blk")
    z = lax.axis_index("wid")
    x = blk // 8
    y = (blk // 2) % 4
    c = blk % 2
    h = z // 2
    l = ((z + 1) // 2) % 2
    twin = h * 2 + (z + 1) % 2
    flip = 3 - z
    far_x, far_y = (x + 2) % 4, (y + 2) % 4

    def dev(xx, yy, cc, zz):
        return ((xx * 4 + yy) * 2 + cc, zz)

    right = (dev(x, (y + 1) % 4, c, z), dev((x + 1) % 4, y, c, z))
    left = (dev(x, (y + 3) % 4, c, z), dev((x + 3) % 4, y, c, z))
    other = dev(x, y, 1 - c, z)
    gathered = (qg, pg)
    pos = (y, x)

    def remote(src, dst, ssem, rsem, device):
        return pltpu.make_async_remote_copy(
            src_ref=src, dst_ref=dst, send_sem=ssem, recv_sem=rsem, device_id=device, device_id_type=MESH
        )

    def arrived(dst, sem):
        pltpu.make_async_copy(dst, dst, sem).wait()

    barrier = pltpu.get_barrier_semaphore()
    peers = [other]
    for dz in (1, 2, 3):
        for cc in (0, 1):
            peers.append(dev(x, y, cc, (z + dz) % 4))
    stat_peers = [other, dev(x, y, c, twin), dev(x, y, 1 - c, twin)]
    for dy in (1, 2, 3):
        for cc in (0, 1):
            for zz in (z, twin):
                peers.append(dev(x, (y + dy) % 4, cc, zz))
                stat_peers.append(peers[-1])
    loss_peers = [dev(x, y, c, flip)]
    for dx in (1, 2, 3):
        for zz in (z, flip):
            peers.append(dev((x + dx) % 4, y, c, zz))
            loss_peers.append(peers[-1])
    for peer in peers:
        pl.semaphore_signal(barrier, inc=1, device_id=peer, device_id_type=MESH)
    pl.semaphore_wait(barrier, len(peers))

    def along_z(start):
        for step in range(4):
            for which in (0, 1):
                d = ORDER_IN[which][step]
                zt = (z + 4 - d) % 4
                owner = zt // 2 if which == 0 else ((zt + 1) // 2) % 2

                @pl.when(owner == c)
                def _():
                    for part in (0, 1):
                        src = (q_hbm, p_hbm)[which].at[:, part * WC:(part + 1) * WC]
                        dst = gathered[which].at[d, rows(pos[which])]
                        copy = remote(src, dst, s1.at[which, d, part], r1.at[which, d], dev(x, y, part, zt))
                        if d == 0:
                            if start:
                                @pl.when(c == part)
                                def _():
                                    pltpu.make_async_copy(src, dst, r1.at[which, d]).start()

                            @pl.when(c != part)
                            def _():
                                copy.start() if start else copy.wait_send()
                        else:
                            copy.start() if start else copy.wait_send()

    along_z(True)

    def to_next(step, start):
        for which in (0, 1):
            d = ORDER_IN[which][step]
            own = gathered[which].at[d, rows(pos[which])]
            if start:
                arrived(own, r1.at[which, d])
            for side, device in ((0, right[which]), (1, left[which])):
                copy = remote(own, own, sn.at[which, d, side], rn.at[which, d, side], device)
                copy.start() if start else copy.wait_send()

    def to_far(step, start):
        for which in (0, 1):
            d = ORDER_IN[which][step]
            for side, device in ((0, right[which]), (1, left[which])):
                origin = (pos[which] + (3 if side == 0 else 1)) % 4
                if start:
                    arrived(gathered[which].at[d, rows(origin)], rn.at[which, d, side])
                part = gathered[which].at[d, rows(origin, HALF, side * HALF)]
                copy = remote(part, part, sf.at[which, d, side], rf.at[which, d, side], device)
                copy.start() if start else copy.wait_send()

    def complete(step):
        for which in (0, 1):
            d = ORDER_IN[which][step]
            for side in (0, 1):
                arrived(gathered[which].at[d, rows((pos[which] + 2) % 4, HALF, side * HALF)], rf.at[which, d, side])

    def scores(d, slot):
        part = lax.dot_general(
            pg[d, rows(slot), :], qg[d], (((1,), (1,)), ((), ())), preferred_element_type=F32
        )
        if d == 0:
            tile[rows(slot), :] = part
        else:
            tile[rows(slot), :] += part

    def all_scores(d):
        pl.loop(0, 4)(lambda slot: scores(d, slot))

    to_next(0, True)
    to_next(1, True)
    to_far(0, True)
    to_next(2, True)
    to_far(1, True)
    complete(0)
    all_scores(0)
    to_next(3, True)
    to_far(2, True)
    complete(1)
    complete(2)
    all_scores(1)
    to_far(3, True)
    all_scores(3)
    complete(3)

    def give_tile(j):
        return remote(
            tile.at[rows(2 * (1 - c) + j)], tile_in.at[pl.ds(j * BR, BR)], sst.at[j], rt.at[j], other
        )

    for j in (0, 1):
        scores(2, 2 * (1 - c) + j)
        give_tile(j).start()
    for j in (0, 1):
        scores(2, 2 * c + j)

    lane = lax.broadcasted_iota(jnp.int32, (1, TILE), 1)
    lanes = lax.broadcasted_iota(jnp.int32, (SUB, TILE), 1)
    subs = lax.broadcasted_iota(jnp.int32, (SUB, TILE), 0)
    eye = lanes - subs

    def diagonal(j):
        return jnp.where((2 * c + j == x) & (h == l), y * BR, -2 * TILE)

    def fold(op, acc, value):
        for k in range(0, SUB, 8):
            acc = op(acc, value[k:k + 8, :])
        return acc

    top = jnp.full((8, TILE), NEG, F32)
    diag = jnp.zeros((8, TILE), F32)
    for j in (0, 1):
        block = ((2 * c + j) * 4 + y) * 2 + l
        allow = None
        for yy in (3, 2, 1, 0):
            mine = (x * 4 + yy) * 2 + h
            flag = jnp.where(mine == block, 1, pairs_ref[mine, block])
            allow = jnp.full((1, TILE), flag, jnp.int32) if allow is None else jnp.where(lane < (yy + 1) * BR, flag, allow)
        allowed = jnp.broadcast_to(allow, (SUB, TILE)) == 1
        start = diagonal(j)
        arrived(tile_in.at[pl.ds(j * BR, BR)], rt.at[j])

        def first(i, carry):
            top, diag = carry
            here = rows(2 * c + j, SUB, i * SUB)
            value = (tile[here, :] + tile_in[pl.ds(pl.multiple_of(j * BR + i * SUB, SUB), SUB), :]) * SCALE
            diag = fold(jnp.add, diag, jnp.where(eye == start + i * SUB, value, 0.0))
            value = jnp.where(allowed, value, NEG)
            tile[here, :] = value
            return fold(jnp.maximum, top, value), diag

        top, diag = lax.fori_loop(0, BR // SUB, first, (top, diag))
    top = jnp.max(top, axis=0, keepdims=True)
    diag = jnp.sum(diag, axis=0, keepdims=True)

    total = jnp.zeros((8, TILE), F32)
    for j in (0, 1):

        def second(i, total):
            here = rows(2 * c + j, SUB, i * SUB)
            value = tile[here, :]
            value = jnp.where(value == NEG, 0.0, jnp.exp(value - top))
            tile[here, :] = value
            return fold(jnp.add, total, value)

        total = lax.fori_loop(0, BR // SUB, second, total)
    total = jnp.sum(total, axis=0, keepdims=True)

    sub = lax.broadcasted_iota(jnp.int32, (8, TILE), 0)
    mine = (y * 2 + l) * 2 + c
    stat[...] = jnp.where(sub == 0, top, jnp.where(sub == 1, total, diag))
    stats[mine] = stat[...]
    stat_copies = [
        remote(stat, stats.at[mine], sstat.at[i], rst.at[mine], peer) for i, peer in enumerate(stat_peers)
    ]
    for copy in stat_copies:
        copy.start()
    for slot in range(16):
        pl.when(slot != mine)(lambda slot=slot: arrived(stats.at[slot], rst.at[slot]))
    highest = stats[0, 0:1, :]
    for slot in range(1, 16):
        highest = jnp.maximum(highest, stats[slot, 0:1, :])
    totals = jnp.zeros((1, TILE), F32)
    positive = jnp.zeros((1, TILE), F32)
    for slot in range(16):
        totals = totals + stats[slot, 1:2, :] * jnp.exp(stats[slot, 0:1, :] - highest)
        positive = positive + stats[slot, 2:3, :]
    factor = jnp.exp(top - highest) / totals

    for j in (0, 1):
        start = diagonal(j)

        def third(i, _):
            here = rows(2 * c + j, SUB, i * SUB)
            value = tile[here, :] * factor - jnp.where(eye == start + i * SUB, 1.0, 0.0)
            wp[here, :] = value.astype(BF16)
            return _

        lax.fori_loop(0, BR // SUB, third, 0)
    my_rows = pl.ds(pl.multiple_of(c * CORE, CORE), CORE)
    give_wp = remote(wp.at[my_rows], wp.at[my_rows], sw.at[0], rw.at[0], other)
    give_wp.start()
    wq[c] = jnp.transpose(wp[my_rows, :])
    give_wq = remote(wq.at[c], wq.at[c], sw.at[1], rw.at[1], other)
    give_wq.start()

    group = x * 2 + h
    lossv[...] = jnp.full((8, 128), jnp.sum(highest + jnp.log(totals) - positive), F32)
    losses[group] = lossv[...]
    loss_copies = [
        remote(lossv, losses.at[group], sl.at[i], rl.at[group], peer) for i, peer in enumerate(loss_peers)
    ]
    for copy in loss_copies:
        copy.start()

    other_rows = pl.ds(pl.multiple_of((1 - c) * CORE, CORE), CORE)
    arrived(wp.at[other_rows], rw.at[0])
    arrived(wq.at[1 - c], rw.at[1])

    def gradient(which, d, slot):
        if which == 1:
            return jnp.dot(wp[rows(slot), :], qg[d], preferred_element_type=F32)
        return jnp.dot(wq[0, rows(slot), :], pg[d, 0:CORE, :], preferred_element_type=F32) + jnp.dot(
            wq[1, rows(slot), :], pg[d, CORE:TILE, :], preferred_element_type=F32
        )

    def far_copy(which, d, side):
        return remote(
            st_f.at[which, d, pl.ds(side * HALF, HALF)], in_f.at[which, d, side],
            sf5.at[which, d, side], rf5.at[which, d, side], (right, left)[side][which],
        )

    def next_copy(which, d, side):
        return remote(
            st_n.at[which, d, side], in_n.at[which, d, side],
            sn5.at[which, d, side], rn5.at[which, d, side], (right, left)[side][which],
        )

    def z_copy(which, d):
        owner = (h, l)[which]
        member = (z % 2, (z + 1) % 2)[which]
        dst = in_z.at[which, member, c]
        return owner, dst, remote(
            st_z.at[which, d], dst, sz.at[which, d], rz.at[which, member, c], dev(x, y, owner, (z + d) % 4)
        )

    def send_far(step):
        for which in (0, 1):
            d = ORDER_OUT[which][step]
            st_f[which, d] = gradient(which, d, (pos[which] + 2) % 4).astype(BF16)
            for side in (0, 1):
                far_copy(which, d, side).start()

    def send_next(step):
        for which in (0, 1):
            d = ORDER_OUT[which][step]
            for side in (0, 1):
                part = gradient(which, d, (pos[which] + (1, 3)[side]) % 4)
                add, keep = slice(side * HALF, (side + 1) * HALF), slice((1 - side) * HALF, (2 - side) * HALF)
                st_n[which, d, side, keep] = part[keep].astype(BF16)
                arrived(in_f.at[which, d, side], rf5.at[which, d, side])
                st_n[which, d, side, add] = (part[add] + in_f[which, d, side].astype(F32)).astype(BF16)
                next_copy(which, d, side).start()

    def send_home(step):
        for which in (0, 1):
            d = ORDER_OUT[which][step]
            part = gradient(which, d, pos[which])
            for side in (0, 1):
                arrived(in_n.at[which, d, side], rn5.at[which, d, side])
                part = part + in_n[which, d, side].astype(F32)
            st_z[which, d] = part.astype(BF16)
            owner, dst, copy = z_copy(which, d)
            if d == 0:
                member = (z % 2, (z + 1) % 2)[which]

                @pl.when(owner == c)
                def _():
                    pltpu.make_async_copy(st_z.at[which, d], dst, rz.at[which, member, c]).start()

                @pl.when(owner != c)
                def _():
                    copy.start()
            else:
                copy.start()

    send_far(0)
    send_far(1)
    send_next(0)
    send_far(2)
    send_next(1)
    send_home(0)
    send_far(3)
    send_next(2)
    send_home(1)
    send_next(3)
    send_home(2)
    send_home(3)

    along_z(False)
    for step in range(4):
        to_next(step, False)
        to_far(step, False)
    for j in (0, 1):
        give_tile(j).wait_send()
    for copy in stat_copies:
        copy.wait_send()
    give_wp.wait_send()
    give_wq.wait_send()
    for copy in loss_copies:
        copy.wait_send()
    for which in (0, 1):
        for d in range(4):
            for side in (0, 1):
                far_copy(which, d, side).wait_send()
                next_copy(which, d, side).wait_send()

    for slot in range(8):
        pl.when(slot != group)(lambda slot=slot: arrived(losses.at[slot], rl.at[slot]))
    loss = losses[0]
    for slot in range(1, 8):
        loss = loss + losses[slot]
    loss_ref[0, 0] = loss[0, 0] / (32 * BR)

    for which, out in ((0, gq_ref), (1, gp_ref)):
        for part in (0, 1):
            for member in (0, 1):
                arrived(in_z.at[which, member, part], rz.at[which, member, part])
            out[:, part * WC:(part + 1) * WC] = (
                in_z[which, 0, part].astype(F32) + in_z[which, 1, part].astype(F32)
            ).astype(BF16)
    for which in (0, 1):
        for d in range(4):
            owner, _, copy = z_copy(which, d)
            if d == 0:
                pl.when(owner != c)(lambda copy=copy: copy.wait_send())
            else:
                copy.wait_send()


def body(queries, passages, pairs):
    dma = pltpu.SemaphoreType.DMA
    loss, grad_queries, grad_passages = pl.pallas_call(
        kernel,
        out_shape=(
            jax.ShapeDtypeStruct((1, 1), F32),
            jax.ShapeDtypeStruct(queries.shape, BF16),
            jax.ShapeDtypeStruct(passages.shape, BF16),
        ),
        in_specs=[
            pl.BlockSpec(memory_space=pl.ANY),
            pl.BlockSpec(memory_space=pl.ANY),
            pl.BlockSpec(memory_space=pltpu.SMEM),
        ],
        out_specs=(
            pl.BlockSpec(memory_space=pltpu.SMEM),
            pl.BlockSpec(memory_space=pltpu.VMEM),
            pl.BlockSpec(memory_space=pltpu.VMEM),
        ),
        scratch_shapes=[
            pltpu.VMEM((4, TILE, WC), BF16),
            pltpu.VMEM((4, TILE, WC), BF16),
            pltpu.VMEM((TILE, TILE), F32),
            pltpu.VMEM((CORE, TILE), F32),
            pltpu.VMEM((TILE, TILE), BF16),
            pltpu.VMEM((2, TILE, CORE), BF16),
            pltpu.VMEM((2, 4, BR, WC), BF16),
            pltpu.VMEM((2, 4, 2, HALF, WC), BF16),
            pltpu.VMEM((2, 4, 2, BR, WC), BF16),
            pltpu.VMEM((2, 4, 2, BR, WC), BF16),
            pltpu.VMEM((2, 4, BR, WC), BF16),
            pltpu.VMEM((2, 2, 2, BR, WC), BF16),
            pltpu.VMEM((8, TILE), F32),
            pltpu.VMEM((16, 8, TILE), F32),
            pltpu.VMEM((8, 128), F32),
            pltpu.VMEM((8, 8, 128), F32),
            dma((2, 4)), dma((2, 4, 2)),
            dma((2, 4, 2)), dma((2, 4, 2)),
            dma((2, 4, 2)), dma((2, 4, 2)),
            dma((2,)), dma((2,)),
            dma((16,)), dma((15,)),
            dma((2,)), dma((2,)),
            dma((2, 4, 2)), dma((2, 4, 2)),
            dma((2, 4, 2)), dma((2, 4, 2)),
            dma((2, 2, 2)), dma((2, 4)),
            dma((8,)), dma((7,)),
        ],
        compiler_params=pltpu.CompilerParams(
            collective_id=0, has_side_effects=True, vmem_limit_bytes=56 * 2**20
        ),
    )(queries, passages, pairs)
    return loss.reshape(()), grad_queries, grad_passages


def solution(mesh):
    return jax.shard_map(
        body,
        mesh=mesh,
        in_specs=(P("blk", "wid"), P("blk", "wid"), P()),
        out_specs=(P(), P("blk", "wid"), P("blk", "wid")),
        check_vma=False,
    )
```

time: 360 us -> 108 us (0.30)
  waiting for transfers between devices: 233 us -> 0 us
  Pallas kernels: 0 us -> 102 us
  blocking collectives: 63.8 us -> 0 us
  matrix products: 38.1 us -> 0 us
  between operations: 15.6 us -> 2.4 us
  other arithmetic: 8.15 us -> 0 us
    psum x1 -> x0, waiting for transfers between devices: 127 us -> none  [body(): scores = lax.psum(partial_value, 'wid') * score_scale]
    pallas_call x0 -> x1, Pallas kernels: none -> 102 us  [body(): pl.pallas_call(kernel, out_shape=(jax.ShapeDtypeStruct((1, 1), F32), jax....]
    all_gather x1 -> x0, waiting for transfers between devices: 73.6 us -> none  [body(): gathered = lax.all_gather(passages, 'blk', axis=0, tiled=True)]
    psum x1 -> x0, blocking collectives: 63.8 us -> none  [body(): loss = lax.psum(loss_part, 'blk') / (blocks * block_rows)]
    dot_general x3 -> x0, matrix products: 38.1 us -> none  [the longest x1 13.4 us: body(): lax.dot_general(weights, queries, (((0,), (0,)), ((), ())), preferred_ele...]
    reduce_scatter x1 -> x0, waiting for transfers between devices: 30.9 us -> none  [body(): lax.psum_scatter(lax.dot_general(weights, queries, (((0,), (0,)), ((), ()...]
    reduce_max x1 -> x0, other arithmetic: 3.86 us -> none  [softmax_weights(): highest = jnp.max(masked, axis=1, keepdims=True)]
  transfers between devices with their start and end apart: 3 -> 0, of which waited for: 3 -> 0; matrix products, arithmetic and copies ran while one was open for 4% -> 0% of each run, Pallas kernels for 0% -> 0%
where the time goes in v1:
time: 108 us; the launch traced here: 107 us
  Pallas kernels  102 us (94%)
  local copies, waits for them, and re-layouts  2.64 us (2%)
  between operations  2.4 us (2%)
    pallas_call x1, Pallas kernels, body(): pl.pallas_call(kernel, out_shape=(jax.ShapeDtypeStruct((1, 1), F32), jax....  102 us
    unnamed x4, local copies, waits for them, and re-layouts  2.64 us

profile of v1, /device:TPU:1, one launch (start us, length us, event | category | flops | bytes accessed | tf_op | source)
XLA Modules:
  0.0 107.0 jit_solution(13170713146078986273)
XLA Ops:
  0.6 102.0 %shard_map.58 = (f32[1,1]{1,0:T(1,128)}, bf16[224,1024]{1,0:T(8,128)(2,1)}, bf16[224,1024]{1,0:T(8,128)(2,1)}) custom-call(bf16[224,1024]{1,0:T(8,128)(2,1)} %q_hbm.1, bf16[224,1024]{1,0:T(8,128)(2,1)} %p_hbm.1, s32[32,32]{1,0:T(8,128)} %pairs_ref.1), custom_call_target="tpu_custom_call" | custom-call | tf_op jit(solution)/shard_map/pallas_call | solution.py:399
  103.2 0.0 copy-start
  103.2 1.9 %copy.10 = bf16[224,1024]{1,0:T(8,128)(2,1)} copy(bf16[224,1024]{1,0:T(8,128)(2,1)} %get-tuple-element.13) | data formatting | bytes 917504
  105.1 0.0 copy-done
  105.1 0.8 copy.11
Async XLA Ops:
  103.2 1.9 %copy-start = (bf16[224,1024]{1,0:T(8,128)(2,1)S(1)}, bf16[224,1024]{1,0:T(8,128)(2,1)}, u32[]{:S(2)}) copy-start(bf16[224,1024]{1,0:T(8,128)(2,1)} %get-tuple-element.14) | copy-start | bytes 1376260

commit v2 on v1

--- a/solution.py
+++ b/solution.py
@@ -25,8 +25,8 @@
 
 
 def kernel(
-    q_hbm, p_hbm, pairs_ref, loss_ref, gq_ref, gp_ref,
-    qg, pg, tile, tile_in, wp, wq, st_f, in_f, st_n, in_n, st_z, in_z, stat, stats, lossv, losses,
+    q_hbm, p_hbm, pairs_ref, loss_ref, in_q, in_p,
+    qg, pg, tile, tile_in, wp, wq, st_f, in_f, st_n, in_n, st_z, stat, stats, lossv, losses,
     r1, s1, rn, sn, rf, sf, rt, sst, rst, sstat, rw, sw, rf5, sf5, rn5, sn5, rz, sz, rl, sl,
 ):
     blk = lax.axis_index("blk")
@@ -77,32 +77,32 @@
         pl.semaphore_signal(barrier, inc=1, device_id=peer, device_id_type=MESH)
     pl.semaphore_wait(barrier, len(peers))
 
-    def along_z(start):
-        for step in range(4):
-            for which in (0, 1):
-                d = ORDER_IN[which][step]
-                zt = (z + 4 - d) % 4
-                owner = zt // 2 if which == 0 else ((zt + 1) // 2) % 2
-
-                @pl.when(owner == c)
-                def _():
-                    for part in (0, 1):
-                        src = (q_hbm, p_hbm)[which].at[:, part * WC:(part + 1) * WC]
-                        dst = gathered[which].at[d, rows(pos[which])]
-                        copy = remote(src, dst, s1.at[which, d, part], r1.at[which, d], dev(x, y, part, zt))
-                        if d == 0:
-                            if start:
-                                @pl.when(c == part)
-                                def _():
-                                    pltpu.make_async_copy(src, dst, r1.at[which, d]).start()
-
-                            @pl.when(c != part)
+    def along_z(step, start):
+        for which in (0, 1):
+            d = ORDER_IN[which][step]
+            zt = (z + 4 - d) % 4
+            owner = zt // 2 if which == 0 else ((zt + 1) // 2) % 2
+
+            @pl.when(owner == c)
+            def _():
+                for part in (0, 1):
+                    src = (q_hbm, p_hbm)[which].at[:, part * WC:(part + 1) * WC]
+                    dst = gathered[which].at[d, rows(pos[which])]
+                    copy = remote(src, dst, s1.at[which, d, part], r1.at[which, d], dev(x, y, part, zt))
+                    if d == 0:
+                        if start:
+                            @pl.when(c == part)
                             def _():
-                                copy.start() if start else copy.wait_send()
-                        else:
+                                pltpu.make_async_copy(src, dst, r1.at[which, d]).start()
+
+                        @pl.when(c != part)
+                        def _():
                             copy.start() if start else copy.wait_send()
-
-    along_z(True)
+                    else:
+                        copy.start() if start else copy.wait_send()
+
+    along_z(0, True)
+    along_z(1, True)
 
     def to_next(step, start):
         for which in (0, 1):
@@ -145,13 +145,17 @@
 
     to_next(0, True)
     to_next(1, True)
+    along_z(1, False)
+    along_z(2, True)
     to_far(0, True)
     to_next(2, True)
+    along_z(2, False)
+    along_z(3, True)
     to_far(1, True)
     complete(0)
     all_scores(0)
+    to_far(2, True)
     to_next(3, True)
-    to_far(2, True)
     complete(1)
     complete(2)
     all_scores(1)
@@ -222,9 +226,16 @@
         total = lax.fori_loop(0, BR // SUB, second, total)
     total = jnp.sum(total, axis=0, keepdims=True)
 
-    sub = lax.broadcasted_iota(jnp.int32, (8, TILE), 0)
+    def pack(row):
+        parts = [row[:, k * 128:(k + 1) * 128] for k in range(TILE // 128)]
+        return jnp.concatenate(parts + [jnp.zeros((1, 128), F32)], axis=0)
+
+    def unpack(block):
+        return jnp.concatenate([block[k:k + 1, :] for k in range(TILE // 128)], axis=1)
+
     mine = (y * 2 + l) * 2 + c
-    stat[...] = jnp.where(sub == 0, top, jnp.where(sub == 1, total, diag))
+    stat[0:8, :] = pack(jnp.where(total > 0, top + jnp.log(total), NEG))
+    stat[8:16, :] = pack(diag)
     stats[mine] = stat[...]
     stat_copies = [
         remote(stat, stats.at[mine], sstat.at[i], rst.at[mine], peer) for i, peer in enumerate(stat_peers)
@@ -233,15 +244,16 @@
         copy.start()
     for slot in range(16):
         pl.when(slot != mine)(lambda slot=slot: arrived(stats.at[slot], rst.at[slot]))
-    highest = stats[0, 0:1, :]
+    highest = stats[0, 0:8, :]
     for slot in range(1, 16):
-        highest = jnp.maximum(highest, stats[slot, 0:1, :])
-    totals = jnp.zeros((1, TILE), F32)
-    positive = jnp.zeros((1, TILE), F32)
+        highest = jnp.maximum(highest, stats[slot, 0:8, :])
+    totals = jnp.zeros((8, 128), F32)
+    positive = jnp.zeros((8, 128), F32)
     for slot in range(16):
-        totals = totals + stats[slot, 1:2, :] * jnp.exp(stats[slot, 0:1, :] - highest)
-        positive = positive + stats[slot, 2:3, :]
-    factor = jnp.exp(top - highest) / totals
+        totals = totals + jnp.exp(stats[slot, 0:8, :] - highest)
+        positive = positive + stats[slot, 8:16, :]
+    log_total = highest + jnp.log(totals)
+    factor = jnp.exp(top - unpack(log_total))
 
     for j in (0, 1):
         start = diagonal(j)
@@ -261,7 +273,8 @@
     give_wq.start()
 
     group = x * 2 + h
-    lossv[...] = jnp.full((8, 128), jnp.sum(highest + jnp.log(totals) - positive), F32)
+    row = lax.broadcasted_iota(jnp.int32, (8, 128), 0)
+    lossv[...] = jnp.full((8, 128), jnp.sum(jnp.where(row < TILE // 128, log_total - positive, 0.0)), F32)
     losses[group] = lossv[...]
     loss_copies = [
         remote(lossv, losses.at[group], sl.at[i], rl.at[group], peer) for i, peer in enumerate(loss_peers)
@@ -271,7 +284,6 @@
 
     other_rows = pl.ds(pl.multiple_of((1 - c) * CORE, CORE), CORE)
     arrived(wp.at[other_rows], rw.at[0])
-    arrived(wq.at[1 - c], rw.at[1])
 
     def gradient(which, d, slot):
         if which == 1:
@@ -295,20 +307,22 @@
     def z_copy(which, d):
         owner = (h, l)[which]
         member = (z % 2, (z + 1) % 2)[which]
-        dst = in_z.at[which, member, c]
+        dst = (in_q, in_p)[which].at[member, :, pl.ds(pl.multiple_of(c * WC, WC), WC)]
         return owner, dst, remote(
             st_z.at[which, d], dst, sz.at[which, d], rz.at[which, member, c], dev(x, y, owner, (z + d) % 4)
         )
 
     def send_far(step):
-        for which in (0, 1):
+        for which in (1, 0):
             d = ORDER_OUT[which][step]
+            if which == 0 and step == 0:
+                arrived(wq.at[1 - c], rw.at[1])
             st_f[which, d] = gradient(which, d, (pos[which] + 2) % 4).astype(BF16)
             for side in (0, 1):
                 far_copy(which, d, side).start()
 
     def send_next(step):
-        for which in (0, 1):
+        for which in (1, 0):
             d = ORDER_OUT[which][step]
             for side in (0, 1):
                 part = gradient(which, d, (pos[which] + (1, 3)[side]) % 4)
@@ -319,7 +333,7 @@
                 next_copy(which, d, side).start()
 
     def send_home(step):
-        for which in (0, 1):
+        for which in (1, 0):
             d = ORDER_OUT[which][step]
             part = gradient(which, d, pos[which])
             for side in (0, 1):
@@ -353,7 +367,8 @@
     send_home(2)
     send_home(3)
 
-    along_z(False)
+    along_z(0, False)
+    along_z(3, False)
     for step in range(4):
         to_next(step, False)
         to_far(step, False)
@@ -378,13 +393,10 @@
         loss = loss + losses[slot]
     loss_ref[0, 0] = loss[0, 0] / (32 * BR)
 
-    for which, out in ((0, gq_ref), (1, gp_ref)):
+    for which in (0, 1):
         for part in (0, 1):
             for member in (0, 1):
-                arrived(in_z.at[which, member, part], rz.at[which, member, part])
-            out[:, part * WC:(part + 1) * WC] = (
-                in_z[which, 0, part].astype(F32) + in_z[which, 1, part].astype(F32)
-            ).astype(BF16)
+                arrived((in_q, in_p)[which].at[member, :, part * WC:(part + 1) * WC], rz.at[which, member, part])
     for which in (0, 1):
         for d in range(4):
             owner, _, copy = z_copy(which, d)
@@ -396,12 +408,12 @@
 
 def body(queries, passages, pairs):
     dma = pltpu.SemaphoreType.DMA
-    loss, grad_queries, grad_passages = pl.pallas_call(
+    loss, in_q, in_p = pl.pallas_call(
         kernel,
         out_shape=(
             jax.ShapeDtypeStruct((1, 1), F32),
-            jax.ShapeDtypeStruct(queries.shape, BF16),
-            jax.ShapeDtypeStruct(passages.shape, BF16),
+            jax.ShapeDtypeStruct((2, *queries.shape), BF16),
+            jax.ShapeDtypeStruct((2, *passages.shape), BF16),
         ),
         in_specs=[
             pl.BlockSpec(memory_space=pl.ANY),
@@ -410,8 +422,8 @@
         ],
         out_specs=(
             pl.BlockSpec(memory_space=pltpu.SMEM),
-            pl.BlockSpec(memory_space=pltpu.VMEM),
-            pl.BlockSpec(memory_space=pltpu.VMEM),
+            pl.BlockSpec(memory_space=pl.ANY),
+            pl.BlockSpec(memory_space=pl.ANY),
         ),
         scratch_shapes=[
             pltpu.VMEM((4, TILE, WC), BF16),
@@ -425,9 +437,8 @@
             pltpu.VMEM((2, 4, 2, BR, WC), BF16),
             pltpu.VMEM((2, 4, 2, BR, WC), BF16),
             pltpu.VMEM((2, 4, BR, WC), BF16),
-            pltpu.VMEM((2, 2, 2, BR, WC), BF16),
-            pltpu.VMEM((8, TILE), F32),
-            pltpu.VMEM((16, 8, TILE), F32),
+            pltpu.VMEM((16, 128), F32),
+            pltpu.VMEM((16, 16, 128), F32),
             pltpu.VMEM((8, 128), F32),
             pltpu.VMEM((8, 8, 128), F32),
             dma((2, 4)), dma((2, 4, 2)),
@@ -445,7 +456,8 @@
             collective_id=0, has_side_effects=True, vmem_limit_bytes=56 * 2**20
         ),
     )(queries, passages, pairs)
-    return loss.reshape(()), grad_queries, grad_passages
+    grads = [(pair[0].astype(F32) + pair[1].astype(F32)).astype(BF16) for pair in (in_q, in_p)]
+    return loss.reshape(()), *grads
 
 
 def solution(mesh):

time: 108 us -> 99.4 us (0.920)
  Pallas kernels: 102 us -> 93.7 us
  other arithmetic: 0 us -> 2.7 us
  local copies, waits for them, and re-layouts: 2.64 us -> 0 us
    pallas_call x1, Pallas kernels: 102 us -> 93.7 us  [body(): pl.pallas_call(kernel, out_shape=(jax.ShapeDtypeStruct((1, 1), F32), jax....]
    convert_element_type x0 -> x1, other arithmetic: none -> 2.7 us  [body(): (pair[0].astype(F32) + pair[1].astype(F32)).astype(BF16)]
    unnamed x4 -> x0, local copies, waits for them, and re-layouts: 2.64 us -> none
where the time goes in v2:
time: 99.4 us; the launch traced here: 98.9 us
  Pallas kernels  93.7 us (94%)
  other arithmetic  2.7 us (3%)
  between operations  2.46 us (2%)
    pallas_call x1, Pallas kernels, body(): pl.pallas_call(kernel, out_shape=(jax.ShapeDtypeStruct((1, 1), F32), jax....  93.7 us
    convert_element_type x1, other arithmetic, body(): (pair[0].astype(F32) + pair[1].astype(F32)).astype(BF16)  2.7 us

profile of v2, /device:TPU:1, one launch (start us, length us, event | category | flops | bytes accessed | tf_op | source)
XLA Modules:
  0.0 98.9 jit_solution(3884677015945328162)
XLA Ops:
  0.6 93.7 %shard_map.58 = (f32[1,1]{1,0:T(1,128)}, bf16[2,224,1024]{2,1,0:T(8,128)(2,1)}, bf16[2,224,1024]{2,1,0:T(8,128)(2,1)}) custom-call(bf16[224,1024]{1,0:T(8,128)(2,1)} %q_hbm.1, bf16[224,1024]{1,0:T(8,128)(2,1)} %p_hbm.1, s32[32,32]{1,0:T(8,128)} %pairs_ref.1), custom_call_target="tpu_custom_call" | custom-call | tf_op jit(solution)/shard_map/pallas_call | solution.py:411
  94.3 2.7 %fusion = (bf16[224,1024]{1,0:T(8,128)(2,1)}, bf16[224,1024]{1,0:T(8,128)(2,1)}) fusion(bf16[2,224,1024]{2,1,0:T(8,128)(2,1)} %get-tuple-element.7, bf16[2,224,1024]{2,1,0:T(8,128)(2,1)} %get-tuple-element.8), kind=kLoop, calls=%fused_computation.2 | loop fusion | flops 1835008 | bytes 2752512 | tf_op jit(solution)/shard_map/convert_element_type | solution.py:459

commit v3 on v2

--- a/solution.py
+++ b/solution.py
@@ -27,7 +27,7 @@
 def kernel(
     q_hbm, p_hbm, pairs_ref, loss_ref, in_q, in_p,
     qg, pg, tile, tile_in, wp, wq, st_f, in_f, st_n, in_n, st_z, stat, stats, lossv, losses,
-    r1, s1, rn, sn, rf, sf, rt, sst, rst, sstat, rw, sw, rf5, sf5, rn5, sn5, rz, sz, rl, sl,
+    r1, s1, s0, rn, sn, rf, sf, rt, sst, rst, sstat, rw, sw, rf5, sf5, rn5, sn5, rz, sz, rl, sl,
 ):
     blk = lax.axis_index("blk")
     z = lax.axis_index("wid")
@@ -59,23 +59,24 @@
 
     barrier = pltpu.get_barrier_semaphore()
     peers = [other]
+    for device in (*right, *left):
+        peers.append(device)
+        peers.append((device[0] + 1 - 2 * c, device[1]))
     for dz in (1, 2, 3):
         for cc in (0, 1):
             peers.append(dev(x, y, cc, (z + dz) % 4))
+    for peer in peers:
+        pl.semaphore_signal(barrier, inc=1, device_id=peer, device_id_type=MESH)
+    pl.semaphore_wait(barrier, len(peers))
     stat_peers = [other, dev(x, y, c, twin), dev(x, y, 1 - c, twin)]
     for dy in (1, 2, 3):
         for cc in (0, 1):
             for zz in (z, twin):
-                peers.append(dev(x, (y + dy) % 4, cc, zz))
-                stat_peers.append(peers[-1])
+                stat_peers.append(dev(x, (y + dy) % 4, cc, zz))
     loss_peers = [dev(x, y, c, flip)]
     for dx in (1, 2, 3):
         for zz in (z, flip):
-            peers.append(dev((x + dx) % 4, y, c, zz))
-            loss_peers.append(peers[-1])
-    for peer in peers:
-        pl.semaphore_signal(barrier, inc=1, device_id=peer, device_id_type=MESH)
-    pl.semaphore_wait(barrier, len(peers))
+            loss_peers.append(dev((x + dx) % 4, y, c, zz))
 
     def along_z(step, start):
         for which in (0, 1):
@@ -90,6 +91,12 @@
                     dst = gathered[which].at[d, rows(pos[which])]
                     copy = remote(src, dst, s1.at[which, d, part], r1.at[which, d], dev(x, y, part, zt))
                     if d == 0:
+                        for side, device in ((0, right[which]), (1, left[which])):
+                            direct = remote(
+                                src, dst, s0.at[which, part, side], rn.at[which, d, side],
+                                (device[0] - c + part, device[1]),
+                            )
+                            direct.start() if start else direct.wait_send()
                         if start:
                             @pl.when(c == part)
                             def _():
@@ -143,7 +150,6 @@
     def all_scores(d):
         pl.loop(0, 4)(lambda slot: scores(d, slot))
 
-    to_next(0, True)
     to_next(1, True)
     along_z(1, False)
     along_z(2, True)
@@ -152,6 +158,8 @@
     along_z(2, False)
     along_z(3, True)
     to_far(1, True)
+    for which in (0, 1):
+        arrived(gathered[which].at[0, rows(pos[which])], r1.at[which, 0])
     complete(0)
     all_scores(0)
     to_far(2, True)
@@ -370,7 +378,8 @@
     along_z(0, False)
     along_z(3, False)
     for step in range(4):
-        to_next(step, False)
+        if step > 0:
+            to_next(step, False)
         to_far(step, False)
     for j in (0, 1):
         give_tile(j).wait_send()
@@ -441,7 +450,7 @@
             pltpu.VMEM((16, 16, 128), F32),
             pltpu.VMEM((8, 128), F32),
             pltpu.VMEM((8, 8, 128), F32),
-            dma((2, 4)), dma((2, 4, 2)),
+            dma((2, 4)), dma((2, 4, 2)), dma((2, 2, 2)),
             dma((2, 4, 2)), dma((2, 4, 2)),
             dma((2, 4, 2)), dma((2, 4, 2)),
             dma((2,)), dma((2,)),

time: 99.4 us -> 98.4 us (0.990); the launches traced: 98.9 us -> 96.7 us
  Pallas kernels: 93.7 us -> 91.5 us
    pallas_call x1, Pallas kernels: 93.7 us -> 91.5 us  [body(): pl.pallas_call(kernel, out_shape=(jax.ShapeDtypeStruct((1, 1), F32), jax....]
where the time goes in v3:
time: 98.4 us; the launch traced here: 96.7 us
  Pallas kernels  91.5 us (93%)
  other arithmetic  2.7 us (3%)
  between operations  2.46 us (2%)
    pallas_call x1, Pallas kernels, body(): pl.pallas_call(kernel, out_shape=(jax.ShapeDtypeStruct((1, 1), F32), jax....  91.5 us
    convert_element_type x1, other arithmetic, body(): (pair[0].astype(F32) + pair[1].astype(F32)).astype(BF16)  2.7 us

profile of v3, /device:TPU:1, one launch (start us, length us, event | category | flops | bytes accessed | tf_op | source)
XLA Modules:
  0.0 96.7 jit_solution(13129814893034775644)
XLA Ops:
  0.6 91.5 %shard_map.58 = (f32[1,1]{1,0:T(1,128)}, bf16[2,224,1024]{2,1,0:T(8,128)(2,1)}, bf16[2,224,1024]{2,1,0:T(8,128)(2,1)}) custom-call(bf16[224,1024]{1,0:T(8,128)(2,1)} %q_hbm.1, bf16[224,1024]{1,0:T(8,128)(2,1)} %p_hbm.1, s32[32,32]{1,0:T(8,128)} %pairs_ref.1), custom_call_target="tpu_custom_call" | custom-call | tf_op jit(solution)/shard_map/pallas_call | solution.py:420
  92.1 2.7 %fusion = (bf16[224,1024]{1,0:T(8,128)(2,1)}, bf16[224,1024]{1,0:T(8,128)(2,1)}) fusion(bf16[2,224,1024]{2,1,0:T(8,128)(2,1)} %get-tuple-element.7, bf16[2,224,1024]{2,1,0:T(8,128)(2,1)} %get-tuple-element.8), kind=kLoop, calls=%fused_computation.2 | loop fusion | flops 1835008 | bytes 2752512 | tf_op jit(solution)/shard_map/convert_element_type | solution.py:468

commit v4 on v3

v4 whole, which is shorter than its diff:
```python
import jax
import jax.numpy as jnp
from jax import lax
from jax.experimental import pallas as pl
from jax.experimental.pallas import tpu as pltpu
from jax.sharding import PartitionSpec as P

MESH = pl.DeviceIdType.MESH
BR = 224
HALF = BR // 2
WC = 512
TILE = 4 * BR
CORE = 2 * BR
SUB = 32
NEG = -1e30
SCALE = 4096 ** -0.5
MC = WC // 2
PAIRED = (0, 2, 1, 3)
F32 = jnp.float32
BF16 = jnp.bfloat16


def rows(slot, n=BR, off=0):
    return pl.ds(pl.multiple_of(slot * BR + off, 16), n)


def kernel(
    q_hbm, p_hbm, pairs_ref, loss_ref, in_q, in_p,
    qg, pg, tile, tile_in, wp, wq, st_f, in_f, st_n, in_n, st_z, st_m, in_m, zero, stat, stats, lossv, losses,
    r1, s1, s0, rn, sn, rf, sf, rt, sst, rst, sstat, rw, sw, rf5, sf5, rn5, sn5, rz, sz, rl, sl, rm, sm, rm5, sm5, s_fill,
):
    blk = lax.axis_index("blk")
    z = lax.axis_index("wid")
    x = blk // 8
    y = (blk // 2) % 4
    c = blk % 2
    h = z // 2
    l = ((z + 1) // 2) % 2
    twin = h * 2 + (z + 1) % 2
    flip = 3 - z
    far_x, far_y = (x + 2) % 4, (y + 2) % 4

    def dev(xx, yy, cc, zz):
        return ((xx * 4 + yy) * 2 + cc, zz)

    right = (dev(x, (y + 1) % 4, c, z), dev((x + 1) % 4, y, c, z))
    left = (dev(x, (y + 3) % 4, c, z), dev((x + 3) % 4, y, c, z))
    other = dev(x, y, 1 - c, z)
    gathered = (qg, pg)
    pos = (y, x)

    def remote(src, dst, ssem, rsem, device):
        return pltpu.make_async_remote_copy(
            src_ref=src, dst_ref=dst, send_sem=ssem, recv_sem=rsem, device_id=device, device_id_type=MESH
        )

    def arrived(dst, sem):
        pltpu.make_async_copy(dst, dst, sem).wait()

    barrier = pltpu.get_barrier_semaphore()
    peers = [other]
    for device in (*right, *left):
        peers.append(device)
        peers.append((device[0] + 1 - 2 * c, device[1]))
    for dz in (1, 2, 3):
        for cc in (0, 1):
            peers.append(dev(x, y, cc, (z + dz) % 4))
    for peer in peers:
        pl.semaphore_signal(barrier, inc=1, device_id=peer, device_id_type=MESH)
    pl.semaphore_wait(barrier, len(peers))
    stat_peers = [dev(x, (y + dy) % 4, cc, zz) for dy in (2, 1, 3) for zz in (twin, z) for cc in (0, 1)]
    stat_peers += [dev(x, y, 0, twin), dev(x, y, 1, twin), other]
    loss_peers = [dev(x, y, c, flip)]
    for dx in (1, 2, 3):
        for zz in (z, flip):
            loss_peers.append(dev((x + dx) % 4, y, c, zz))

    turn = 1 - 2 * (z % 2)

    def z_of(which, slot):
        step = (turn, -turn)[which]
        return (z + 4 + (0, -step, step, 2)[slot]) % 4

    def holds(which, zz):
        return zz // 2 if which == 0 else ((zz + 1) // 2) % 2

    def cols(slot, start=0):
        return slice(start + (MC if slot == 3 else 0), start + WC)

    def member(which, zz):
        return (zz % 2, (zz + 1) % 2)[which]

    def lacks(which, one):
        return (holds(which, z) != c) & (member(which, z) == one)

    def fill(start):
        for which in (0, 1):
            for one in (0, 1):

                @pl.when(lacks(which, one))
                def _():
                    for part in (0, 1):
                        dst = (in_q, in_p)[which].at[one, :, part * WC:part * WC + MC]
                        copy = pltpu.make_async_copy(zero, dst, s_fill.at[which, part])
                        copy.start() if start else copy.wait()

    def along_z(slot, start):
        for which in (0, 1):
            zt = z_of(which, slot)

            @pl.when(holds(which, zt) == c)
            def _():
                for part in (0, 1):
                    src = (q_hbm, p_hbm)[which].at[:, cols(slot, part * WC)]
                    dst = gathered[which].at[slot, rows(pos[which]), cols(slot)]
                    copy = remote(src, dst, s1.at[which, slot, part], r1.at[which, slot], dev(x, y, part, zt))
                    if slot == 0:
                        for half in (0, 1):
                            for side, device in ((0, right[which]), (1, left[which])):
                                off = (side, 1 - side)[half] * HALF
                                direct = remote(
                                    (q_hbm, p_hbm)[which].at[off:off + HALF, cols(slot, part * WC)],
                                    gathered[which].at[slot, rows(pos[which], HALF, off), cols(slot)],
                                    s0.at[which, part, side, half], rn.at[which, slot, side, half],
                                    (device[0] - c + part, device[1]),
                                )
                                direct.start() if start else direct.wait_send()
                        if start:
                            @pl.when(c == part)
                            def _():
                                pltpu.make_async_copy(src, dst, r1.at[which, slot]).start()

                        @pl.when(c != part)
                        def _():
                            copy.start() if start else copy.wait_send()
                    else:
                        copy.start() if start else copy.wait_send()

    def to_next(slot, start):
        for which in (0, 1):
            own = gathered[which].at[slot, rows(pos[which]), cols(slot)]
            if start:
                arrived(own, r1.at[which, slot])
            for half in (0, 1):
                for side, device in ((0, right[which]), (1, left[which])):
                    part = gathered[which].at[slot, rows(pos[which], HALF, (side, 1 - side)[half] * HALF), cols(slot)]
                    copy = remote(part, part, sn.at[which, slot, side, half], rn.at[which, slot, side, half], device)
                    copy.start() if start else copy.wait_send()

    def from_next(which, slot, side, half):
        origin = (pos[which] + (3, 1)[side]) % 4
        part = gathered[which].at[slot, rows(origin, HALF, (side, 1 - side)[half] * HALF), cols(slot)]
        return part, rn.at[which, slot, side, half]

    def to_far(slot, start):
        for which in (0, 1):
            for side, device in ((0, right[which]), (1, left[which])):
                part, came = from_next(which, slot, side, 0)
                if start:
                    arrived(part, came)
                copy = remote(part, part, sf.at[which, slot, side], rf.at[which, slot, side], device)
                copy.start() if start else copy.wait_send()

    def rest_of_next(slot):
        for which in (0, 1):
            for side in (0, 1):
                arrived(*from_next(which, slot, side, 1))

    def from_far(slot):
        for which in (0, 1):
            for side in (0, 1):
                far = rows((pos[which] + 2) % 4, HALF, side * HALF)
                arrived(gathered[which].at[slot, far, cols(slot)], rf.at[which, slot, side])

    mates = [dev(x, y, c, z_of(which, 2)) for which in (0, 1)]

    def to_mate(start, steps=(0, 1, 2, 3)):
        for which in (0, 1):
            for step in steps:
                block = (pos[which] + step) % 4
                copy = remote(
                    gathered[which].at[1, rows(block), 0:MC], gathered[which].at[3, rows(block), 0:MC],
                    sm.at[which, block], rm.at[which, block], mates[which],
                )
                copy.start() if start else copy.wait_send()

    def scores(slot, block):
        part = lax.dot_general(
            pg[PAIRED[slot], rows(block), :], qg[slot], (((1,), (1,)), ((), ())), preferred_element_type=F32
        )
        if slot == 0:
            tile[rows(block), :] = part
        else:
            tile[rows(block), :] += part

    def all_scores(slot):
        pl.loop(0, 4)(lambda block: scores(slot, block))

    along_z(0, True)
    along_z(1, True)
    along_z(2, True)
    zero[...] = jnp.zeros((BR, MC), BF16)
    fill(True)
    to_far(0, True)
    to_next(1, True)
    along_z(3, True)
    to_mate(True, (0,))
    to_next(2, True)
    to_far(1, True)
    rest_of_next(1)
    to_mate(True, (1, 3))
    for which in (0, 1):
        arrived(gathered[which].at[0, rows(pos[which])], r1.at[which, 0])
    rest_of_next(0)
    from_far(0)
    all_scores(0)
    to_far(2, True)
    to_next(3, True)
    from_far(1)
    to_mate(True, (2,))
    rest_of_next(2)
    from_far(2)
    all_scores(1)
    to_far(3, True)
    all_scores(2)
    rest_of_next(3)
    from_far(3)
    for which in (0, 1):
        for block in range(4):
            arrived(gathered[which].at[3, rows(block), 0:MC], rm.at[which, block])

    def give_tile(j):
        return remote(
            tile.at[rows(2 * (1 - c) + j)], tile_in.at[pl.ds(j * BR, BR)], sst.at[j], rt.at[j], other
        )

    for j in (0, 1):
        scores(3, 2 * (1 - c) + j)
        give_tile(j).start()
    for j in (0, 1):
        scores(3, 2 * c + j)

    lane = lax.broadcasted_iota(jnp.int32, (1, TILE), 1)
    lanes = lax.broadcasted_iota(jnp.int32, (SUB, TILE), 1)
    subs = lax.broadcasted_iota(jnp.int32, (SUB, TILE), 0)
    eye = lanes - subs

    def diagonal(j):
        return jnp.where((2 * c + j == x) & (h == l), y * BR, -2 * TILE)

    def fold(op, acc, value):
        for k in range(0, SUB, 8):
            acc = op(acc, value[k:k + 8, :])
        return acc

    top = jnp.full((8, TILE), NEG, F32)
    diag = jnp.zeros((8, TILE), F32)
    for j in (0, 1):
        block = ((2 * c + j) * 4 + y) * 2 + l
        allow = None
        for yy in (3, 2, 1, 0):
            mine = (x * 4 + yy) * 2 + h
            flag = jnp.where(mine == block, 1, pairs_ref[mine, block])
            allow = jnp.full((1, TILE), flag, jnp.int32) if allow is None else jnp.where(lane < (yy + 1) * BR, flag, allow)
        allowed = jnp.broadcast_to(allow, (SUB, TILE)) == 1
        start = diagonal(j)
        arrived(tile_in.at[pl.ds(j * BR, BR)], rt.at[j])

        def first(i, carry):
            top, diag = carry
            here = rows(2 * c + j, SUB, i * SUB)
            value = (tile[here, :] + tile_in[pl.ds(pl.multiple_of(j * BR + i * SUB, SUB), SUB), :]) * SCALE
            diag = fold(jnp.add, diag, jnp.where(eye == start + i * SUB, value, 0.0))
            value = jnp.where(allowed, value, NEG)
            tile[here, :] = value
            return fold(jnp.maximum, top, value), diag

        top, diag = lax.fori_loop(0, BR // SUB, first, (top, diag))
    top = jnp.max(top, axis=0, keepdims=True)
    diag = jnp.sum(diag, axis=0, keepdims=True)

    total = jnp.zeros((8, TILE), F32)
    for j in (0, 1):

        def second(i, total):
            here = rows(2 * c + j, SUB, i * SUB)
            value = tile[here, :]
            value = jnp.where(value == NEG, 0.0, jnp.exp(value - top))
            tile[here, :] = value
            return fold(jnp.add, total, value)

        total = lax.fori_loop(0, BR // SUB, second, total)
    total = jnp.sum(total, axis=0, keepdims=True)

    def pack(row):
        parts = [row[:, k * 128:(k + 1) * 128] for k in range(TILE // 128)]
        return jnp.concatenate(parts + [jnp.zeros((1, 128), F32)], axis=0)

    def unpack(block):
        return jnp.concatenate([block[k:k + 1, :] for k in range(TILE // 128)], axis=1)

    mine = (y * 2 + l) * 2 + c
    stat[0:8, :] = pack(jnp.where(total > 0, top + jnp.log(total), NEG))
    stat[8:16, :] = pack(diag)
    stats[mine] = stat[...]
    stat_copies = [
        remote(stat, stats.at[mine], sstat.at[i], rst.at[mine], peer) for i, peer in enumerate(stat_peers)
    ]
    for copy in stat_copies:
        copy.start()
    for slot in range(16):
        pl.when(slot != mine)(lambda slot=slot: arrived(stats.at[slot], rst.at[slot]))
    highest = stats[0, 0:8, :]
    for slot in range(1, 16):
        highest = jnp.maximum(highest, stats[slot, 0:8, :])
    totals = jnp.zeros((8, 128), F32)
    positive = jnp.zeros((8, 128), F32)
    for slot in range(16):
        totals = totals + jnp.exp(stats[slot, 0:8, :] - highest)
        positive = positive + stats[slot, 8:16, :]
    log_total = highest + jnp.log(totals)
    factor = jnp.exp(top - unpack(log_total))

    def give_wp(j):
        part = wp.at[rows(2 * c + j)]
        return remote(part, part, sw.at[j], rw.at[j], other)

    for j in (0, 1):
        start = diagonal(j)

        def third(i, _):
            here = rows(2 * c + j, SUB, i * SUB)
            value = tile[here, :] * factor - jnp.where(eye == start + i * SUB, 1.0, 0.0)
            wp[here, :] = value.astype(BF16)
            return _

        lax.fori_loop(0, BR // SUB, third, 0)
        give_wp(j).start()
    my_rows = pl.ds(pl.multiple_of(c * CORE, CORE), CORE)
    wq[c] = jnp.transpose(wp[my_rows, :])
    give_wq = remote(wq.at[c], wq.at[c], sw.at[2], rw.at[2], other)
    give_wq.start()

    group = x * 2 + h
    row = lax.broadcasted_iota(jnp.int32, (8, 128), 0)
    lossv[...] = jnp.full((8, 128), jnp.sum(jnp.where(row < TILE // 128, log_total - positive, 0.0)), F32)
    losses[group] = lossv[...]
    loss_copies = [
        remote(lossv, losses.at[group], sl.at[i], rl.at[group], peer) for i, peer in enumerate(loss_peers)
    ]
    for copy in loss_copies:
        copy.start()

    for j in (0, 1):
        arrived(wp.at[rows(2 * (1 - c) + j)], rw.at[j])

    def gradient(which, slot, block, span):
        if which == 1:
            return jnp.dot(wp[rows(block), :], qg[PAIRED[slot], :, span], preferred_element_type=F32)
        return jnp.dot(wq[0, rows(block), :], pg[PAIRED[slot], 0:CORE, span], preferred_element_type=F32) + jnp.dot(
            wq[1, rows(block), :], pg[PAIRED[slot], CORE:TILE, span], preferred_element_type=F32
        )

    def total_of(which, slot, block):
        part = gradient(which, slot, block, cols(slot))
        if slot == 1:
            arrived(in_m.at[which, block], rm5.at[which, block])
            part = jnp.concatenate([part[:, 0:MC] + in_m[which, block].astype(F32), part[:, MC:WC]], axis=1)
        return part

    def far_copy(which, slot, side):
        return remote(
            st_f.at[which, slot, pl.ds(side * HALF, HALF), cols(slot)], in_f.at[which, slot, side, :, cols(slot)],
            sf5.at[which, slot, side], rf5.at[which, slot, side], (right, left)[side][which],
        )

    def next_copy(which, slot, side, half):
        off = (1 - side, side)[half] * HALF
        return remote(
            st_n.at[which, slot, side, pl.ds(off, HALF), cols(slot)],
            in_n.at[which, slot, side, pl.ds(off, HALF), cols(slot)],
            sn5.at[which, slot, side, half], rn5.at[which, slot, side, half], (right, left)[side][which],
        )

    def mate_copy(which, block):
        return remote(
            st_m.at[which, block], in_m.at[which, block], sm5.at[which, block], rm5.at[which, block], mates[which]
        )

    def z_copy(which, slot):
        owner = holds(which, z)
        first = c * WC + (MC if slot == 3 else 0)
        span = pl.ds(pl.multiple_of(first, MC), WC - MC if slot == 3 else WC)
        dst = (in_q, in_p)[which].at[member(which, z), :, span]
        return owner, dst, remote(
            st_z.at[which, slot, :, cols(slot)], dst, sz.at[which, slot], rz.at[which, member(which, z), c],
            dev(x, y, owner, z_of(which, slot)),
        )

    def send_mate():
        for which in (1, 0):
            for step in (2, 1, 3, 0):
                block = (pos[which] + step) % 4
                st_m[which, block] = gradient(which, 3, block, slice(0, MC)).astype(BF16)
                mate_copy(which, block).start()

    def send_far(slot):
        for which in (1, 0):
            if which == 0 and slot == 2:
                arrived(wq.at[1 - c], rw.at[2])
            st_f[which, slot, :, cols(slot)] = total_of(which, slot, (pos[which] + 2) % 4).astype(BF16)
            for side in (0, 1):
                far_copy(which, slot, side).start()

    def send_next(slot):
        for which in (1, 0):
            for side in (0, 1):
                part = total_of(which, slot, (pos[which] + (1, 3)[side]) % 4)
                add, keep = slice(side * HALF, (side + 1) * HALF), slice((1 - side) * HALF, (2 - side) * HALF)
                st_n[which, slot, side, keep, cols(slot)] = part[keep].astype(BF16)
                next_copy(which, slot, side, 0).start()
                arrived(in_f.at[which, slot, side, :, cols(slot)], rf5.at[which, slot, side])
                st_n[which, slot, side, add, cols(slot)] = (
                    part[add] + in_f[which, slot, side, :, cols(slot)].astype(F32)
                ).astype(BF16)
                next_copy(which, slot, side, 1).start()

    def send_home(slot):
        for which in (1, 0):
            part = total_of(which, slot, pos[which])
            for side in (0, 1):
                for half in (0, 1):
                    off = (1 - side, side)[half] * HALF
                    arrived(in_n.at[which, slot, side, pl.ds(off, HALF), cols(slot)], rn5.at[which, slot, side, half])
                part = part + in_n[which, slot, side, :, cols(slot)].astype(F32)
            st_z[which, slot, :, cols(slot)] = part.astype(BF16)
            owner, dst, copy = z_copy(which, slot)
            if slot == 0:

                @pl.when(owner == c)
                def _():
                    pltpu.make_async_copy(st_z.at[which, slot], dst, rz.at[which, member(which, z), c]).start()

                @pl.when(owner != c)
                def _():
                    copy.start()
            else:
                copy.start()

    send_far(2)
    send_far(3)
    send_far(0)
    send_mate()
    send_next(2)
    send_next(3)
    send_far(1)
    send_home(2)
    send_next(1)
    send_home(3)
    send_next(0)
    send_home(1)
    send_home(0)

    to_mate(False)
    for slot in range(4):
        along_z(slot, False)
        if slot > 0:
            to_next(slot, False)
        to_far(slot, False)
    for j in (0, 1):
        give_tile(j).wait_send()
    for copy in stat_copies:
        copy.wait_send()
    for j in (0, 1):
        give_wp(j).wait_send()
    give_wq.wait_send()
    for copy in loss_copies:
        copy.wait_send()
    for which in (0, 1):
        for slot in range(4):
            mate_copy(which, slot).wait_send()
            for side in (0, 1):
                far_copy(which, slot, side).wait_send()
                for half in (0, 1):
                    next_copy(which, slot, side, half).wait_send()

    for slot in range(8):
        pl.when(slot != group)(lambda slot=slot: arrived(losses.at[slot], rl.at[slot]))
    loss = losses[0]
    for slot in range(1, 8):
        loss = loss + losses[slot]
    loss_ref[0, 0] = loss[0, 0] / (32 * BR)

    for which in (0, 1):
        for part in (0, 1):
            for one in (0, 1):
                whole = (in_q, in_p)[which].at[one, :, part * WC:(part + 1) * WC]
                rest = (in_q, in_p)[which].at[one, :, cols(3, part * WC)]
                half = lacks(which, one)
                pl.when(half)(lambda rest=rest, one=one, part=part, which=which: arrived(rest, rz.at[which, one, part]))
                pl.when(jnp.logical_not(half))(
                    lambda whole=whole, one=one, part=part, which=which: arrived(whole, rz.at[which, one, part])
                )
    fill(False)
    for which in (0, 1):
        for slot in range(4):
            owner, _, copy = z_copy(which, slot)
            if slot == 0:
                pl.when(owner != c)(lambda copy=copy: copy.wait_send())
            else:
                copy.wait_send()


def body(queries, passages, pairs):
    dma = pltpu.SemaphoreType.DMA
    loss, in_q, in_p = pl.pallas_call(
        kernel,
        out_shape=(
            jax.ShapeDtypeStruct((1, 1), F32),
            jax.ShapeDtypeStruct((2, *queries.shape), BF16),
            jax.ShapeDtypeStruct((2, *passages.shape), BF16),
        ),
        in_specs=[
            pl.BlockSpec(memory_space=pl.ANY),
            pl.BlockSpec(memory_space=pl.ANY),
            pl.BlockSpec(memory_space=pltpu.SMEM),
        ],
        out_specs=(
            pl.BlockSpec(memory_space=pltpu.SMEM),
            pl.BlockSpec(memory_space=pl.ANY),
            pl.BlockSpec(memory_space=pl.ANY),
        ),
        scratch_shapes=[
            pltpu.VMEM((4, TILE, WC), BF16),
            pltpu.VMEM((4, TILE, WC), BF16),
            pltpu.VMEM((TILE, TILE), F32),
            pltpu.VMEM((CORE, TILE), F32),
            pltpu.VMEM((TILE, TILE), BF16),
            pltpu.VMEM((2, TILE, CORE), BF16),
            pltpu.VMEM((2, 4, BR, WC), BF16),
            pltpu.VMEM((2, 4, 2, HALF, WC), BF16),
            pltpu.VMEM((2, 4, 2, BR, WC), BF16),
            pltpu.VMEM((2, 4, 2, BR, WC), BF16),
            pltpu.VMEM((2, 4, BR, WC), BF16),
            pltpu.VMEM((2, 4, BR, MC), BF16),
            pltpu.VMEM((2, 4, BR, MC), BF16),
            pltpu.VMEM((BR, MC), BF16),
            pltpu.VMEM((16, 128), F32),
            pltpu.VMEM((16, 16, 128), F32),
            pltpu.VMEM((8, 128), F32),
            pltpu.VMEM((8, 8, 128), F32),
            dma((2, 4)), dma((2, 4, 2)), dma((2, 2, 2, 2)),
            dma((2, 4, 2, 2)), dma((2, 4, 2, 2)),
            dma((2, 4, 2)), dma((2, 4, 2)),
            dma((2,)), dma((2,)),
            dma((16,)), dma((15,)),
            dma((3,)), dma((3,)),
            dma((2, 4, 2)), dma((2, 4, 2)),
            dma((2, 4, 2, 2)), dma((2, 4, 2, 2)),
            dma((2, 2, 2)), dma((2, 4)),
            dma((8,)), dma((7,)),
            dma((2, 4)), dma((2, 4)),
            dma((2, 4)), dma((2, 4)),
            dma((2, 2)),
        ],
        compiler_params=pltpu.CompilerParams(
            collective_id=0, has_side_effects=True, vmem_limit_bytes=56 * 2**20
        ),
    )(queries, passages, pairs)
    grads = [(pair[0].astype(F32) + pair[1].astype(F32)).astype(BF16) for pair in (in_q, in_p)]
    return loss.reshape(()), *grads


def solution(mesh):
    return jax.shard_map(
        body,
        mesh=mesh,
        in_specs=(P("blk", "wid"), P("blk", "wid"), P()),
        out_specs=(P(), P("blk", "wid"), P("blk", "wid")),
        check_vma=False,
    )
```

time: 98.4 us -> 93.5 us (0.950); the launches traced: 96.7 us -> 93.2 us
  Pallas kernels: 91.5 us -> 88.1 us
    pallas_call x1, Pallas kernels: 91.5 us -> 88.1 us  [body(): pl.pallas_call(kernel, out_shape=(jax.ShapeDtypeStruct((1, 1), F32), jax....]
where the time goes in v4:
time: 93.5 us; the launch traced here: 93.2 us
  Pallas kernels  88.1 us (94%)
  other arithmetic  2.7 us (3%)
  between operations  2.46 us (3%)
    pallas_call x1, Pallas kernels, body(): pl.pallas_call(kernel, out_shape=(jax.ShapeDtypeStruct((1, 1), F32), jax....  88.1 us
    convert_element_type x1, other arithmetic, body(): (pair[0].astype(F32) + pair[1].astype(F32)).astype(BF16)  2.7 us

profile of v4, /device:TPU:1, one launch (start us, length us, event | category | flops | bytes accessed | tf_op | source)
XLA Modules:
  0.0 93.2 jit_solution(9226141925020188108)
XLA Ops:
  0.6 88.1 %shard_map.58 = (f32[1,1]{1,0:T(1,128)}, bf16[2,224,1024]{2,1,0:T(8,128)(2,1)}, bf16[2,224,1024]{2,1,0:T(8,128)(2,1)}) custom-call(bf16[224,1024]{1,0:T(8,128)(2,1)} %q_hbm.1, bf16[224,1024]{1,0:T(8,128)(2,1)} %p_hbm.1, s32[32,32]{1,0:T(8,128)} %pairs_ref.1), custom_call_target="tpu_custom_call" | custom-call | tf_op jit(solution)/shard_map/pallas_call | solution.py:516
  88.7 2.7 %fusion = (bf16[224,1024]{1,0:T(8,128)(2,1)}, bf16[224,1024]{1,0:T(8,128)(2,1)}) fusion(bf16[2,224,1024]{2,1,0:T(8,128)(2,1)} %get-tuple-element.7, bf16[2,224,1024]{2,1,0:T(8,128)(2,1)} %get-tuple-element.8), kind=kLoop, calls=%fused_computation.2 | loop fusion | flops 1835008 | bytes 2752512 | tf_op jit(solution)/shard_map/convert_element_type | solution.py:570

commit v5 on v4

--- a/solution.py
+++ b/solution.py
@@ -14,7 +14,7 @@
 SUB = 32
 NEG = -1e30
 SCALE = 4096 ** -0.5
-MC = WC // 2
+MC = 384
 PAIRED = (0, 2, 1, 3)
 F32 = jnp.float32
 BF16 = jnp.bfloat16
@@ -338,8 +338,6 @@
         give_wp(j).start()
     my_rows = pl.ds(pl.multiple_of(c * CORE, CORE), CORE)
     wq[c] = jnp.transpose(wp[my_rows, :])
-    give_wq = remote(wq.at[c], wq.at[c], sw.at[2], rw.at[2], other)
-    give_wq.start()
 
     group = x * 2 + h
     row = lax.broadcasted_iota(jnp.int32, (8, 128), 0)
@@ -390,7 +388,7 @@
     def z_copy(which, slot):
         owner = holds(which, z)
         first = c * WC + (MC if slot == 3 else 0)
-        span = pl.ds(pl.multiple_of(first, MC), WC - MC if slot == 3 else WC)
+        span = pl.ds(pl.multiple_of(first, 128), WC - MC if slot == 3 else WC)
         dst = (in_q, in_p)[which].at[member(which, z), :, span]
         return owner, dst, remote(
             st_z.at[which, slot, :, cols(slot)], dst, sz.at[which, slot], rz.at[which, member(which, z), c],
@@ -407,7 +405,7 @@
     def send_far(slot):
         for which in (1, 0):
             if which == 0 and slot == 2:
-                arrived(wq.at[1 - c], rw.at[2])
+                wq[1 - c] = jnp.transpose(wp[pl.ds(pl.multiple_of((1 - c) * CORE, CORE), CORE), :])
             st_f[which, slot, :, cols(slot)] = total_of(which, slot, (pos[which] + 2) % 4).astype(BF16)
             for side in (0, 1):
                 far_copy(which, slot, side).start()
@@ -473,7 +471,6 @@
         copy.wait_send()
     for j in (0, 1):
         give_wp(j).wait_send()
-    give_wq.wait_send()
     for copy in loss_copies:
         copy.wait_send()
     for which in (0, 1):
@@ -554,7 +551,7 @@
             dma((2, 4, 2)), dma((2, 4, 2)),
             dma((2,)), dma((2,)),
             dma((16,)), dma((15,)),
-            dma((3,)), dma((3,)),
+            dma((2,)), dma((2,)),
             dma((2, 4, 2)), dma((2, 4, 2)),
             dma((2, 4, 2, 2)), dma((2, 4, 2, 2)),
             dma((2, 2, 2)), dma((2, 4)),

time: 93.5 us -> 92.8 us (level)
  no operation moved by 1% of the time
where the time goes in v5:
time: 92.8 us; the launch traced here: 92.6 us
  Pallas kernels  87.4 us (94%)
  other arithmetic  2.7 us (3%)
  between operations  2.46 us (3%)
    pallas_call x1, Pallas kernels, body(): pl.pallas_call(kernel, out_shape=(jax.ShapeDtypeStruct((1, 1), F32), jax....  87.4 us
    convert_element_type x1, other arithmetic, body(): (pair[0].astype(F32) + pair[1].astype(F32)).astype(BF16)  2.7 us

profile of v5, /device:TPU:1, one launch (start us, length us, event | category | flops | bytes accessed | tf_op | source)
XLA Modules:
  0.0 92.6 jit_solution(9987693882642726283)
XLA Ops:
  0.6 87.4 %shard_map.58 = (f32[1,1]{1,0:T(1,128)}, bf16[2,224,1024]{2,1,0:T(8,128)(2,1)}, bf16[2,224,1024]{2,1,0:T(8,128)(2,1)}) custom-call(bf16[224,1024]{1,0:T(8,128)(2,1)} %q_hbm.1, bf16[224,1024]{1,0:T(8,128)(2,1)} %p_hbm.1, s32[32,32]{1,0:T(8,128)} %pairs_ref.1), custom_call_target="tpu_custom_call" | custom-call | tf_op jit(solution)/shard_map/pallas_call | solution.py:513
  88.0 2.7 %fusion = (bf16[224,1024]{1,0:T(8,128)(2,1)}, bf16[224,1024]{1,0:T(8,128)(2,1)}) fusion(bf16[2,224,1024]{2,1,0:T(8,128)(2,1)} %get-tuple-element.7, bf16[2,224,1024]{2,1,0:T(8,128)(2,1)} %get-tuple-element.8), kind=kLoop, calls=%fused_computation.2 | loop fusion | flops 1835008 | bytes 2752512 | tf_op jit(solution)/shard_map/convert_element_type | solution.py:567

commit v6 on v5

--- a/solution.py
+++ b/solution.py
@@ -213,15 +213,15 @@
         arrived(gathered[which].at[0, rows(pos[which])], r1.at[which, 0])
     rest_of_next(0)
     from_far(0)
-    all_scores(0)
     to_far(2, True)
     to_next(3, True)
+    all_scores(0)
     from_far(1)
     to_mate(True, (2,))
     rest_of_next(2)
     from_far(2)
+    to_far(3, True)
     all_scores(1)
-    to_far(3, True)
     all_scores(2)
     rest_of_next(3)
     from_far(3)

time: 92.8 us -> 92.7 us (level)
  no operation moved by 1% of the time
where the time goes in v6:
time: 92.7 us; the launch traced here: 92.5 us
  Pallas kernels  87.3 us (94%)
  other arithmetic  2.7 us (3%)
  between operations  2.46 us (3%)
    pallas_call x1, Pallas kernels, body(): pl.pallas_call(kernel, out_shape=(jax.ShapeDtypeStruct((1, 1), F32), jax....  87.3 us
    convert_element_type x1, other arithmetic, body(): (pair[0].astype(F32) + pair[1].astype(F32)).astype(BF16)  2.7 us

profile of v6, /device:TPU:1, one launch (start us, length us, event | category | flops | bytes accessed | tf_op | source)
XLA Modules:
  0.0 92.5 jit_solution(17919473738237510275)
XLA Ops:
  0.6 87.3 %shard_map.58 = (f32[1,1]{1,0:T(1,128)}, bf16[2,224,1024]{2,1,0:T(8,128)(2,1)}, bf16[2,224,1024]{2,1,0:T(8,128)(2,1)}) custom-call(bf16[224,1024]{1,0:T(8,128)(2,1)} %q_hbm.1, bf16[224,1024]{1,0:T(8,128)(2,1)} %p_hbm.1, s32[32,32]{1,0:T(8,128)} %pairs_ref.1), custom_call_target="tpu_custom_call" | custom-call | tf_op jit(solution)/shard_map/pallas_call | solution.py:513
  87.9 2.7 %fusion = (bf16[224,1024]{1,0:T(8,128)(2,1)}, bf16[224,1024]{1,0:T(8,128)(2,1)}) fusion(bf16[2,224,1024]{2,1,0:T(8,128)(2,1)} %get-tuple-element.7, bf16[2,224,1024]{2,1,0:T(8,128)(2,1)} %get-tuple-element.8), kind=kLoop, calls=%fused_computation.2 | loop fusion | flops 1835008 | bytes 2752512 | tf_op jit(solution)/shard_map/convert_element_type | solution.py:567
